TPU v7x, 32 devices: a whole 2x2x4 slice. The times are simulated.
32 devices in a mesh: vid: 4 (over z), ty: 2 (over y), tx: 4 (over x, core).
Axes of the slice: x: 2, y: 2, z: 4, core: 2. Of those that a mesh axis runs over, the one named last changes fastest.
Arguments:
- latent_shards: bfloat16 [4, 99328], P('vid', ('ty', 'tx')), may hold values from -6 to 6
- shard_starts: int32 [4, 9], P('vid'), may hold values from 0 to 4096, as said below
- frame_dims: int32 [4, 2], P('vid'), may hold values from 16 to 128, as said below
- latent_cache: bfloat16 [4, 2, 32, 2048], P('vid', None, 'ty', 'tx'), may hold values from -6 to 6
- feature_cache: bfloat16 [4, 2, 32, 49152], P('vid', None, 'ty', 'tx'), may hold values from -5 to 5
- in_weight: bfloat16 [432, 384], replicated, may hold values from -0.3125 to 0.3125
- in_bias: float32 [384], replicated, may hold values from -3 to 3
- norm_gain: float32 [384], replicated, may hold values from 0.1 to 1.9
- res_weight: bfloat16 [10368, 384], replicated, may hold values from -0.0625 to 0.0625
- res_bias: float32 [384], replicated, may hold values from -3 to 3
- up_weight: bfloat16 [3456, 192], replicated, may hold values from -0.109375 to 0.109375
- up_bias: float32 [192], replicated, may hold values from -3 to 3
Outputs:
- decoded: bfloat16 [4, 64, 49152], P('vid', 'ty', 'tx')
Inputs may be any that keep to these rules, and one draw needn't show every extreme that they name: `frame_dims`: row i gives video i's height, from 16 to 32, and width, from 64 to 128; one video fills the whole canvas and another is exactly 16 by 64. `shard_starts`: row i starts at 0, never falls, ends at video i's height times width, and every shard's token count fits its 776 slots; tokens lie in row-major order of the frame.
All inputs are finite; a program needn't handle non-finite values.
Results may differ from a plain program's by a relative error of at most 0.0095.
Values may be sent and summed in bfloat16 or wider, within the bound.
A program may use at most 64 MiB of HBM per device.

v0:
```python
import jax
import jax.numpy as jnp
from jax import lax
from jax.sharding import PartitionSpec as P

EPS = 1e-06


def padded_2(value, sides, width):
    for axis, dim in sides:
        size, length = (lax.axis_size(axis), value.shape[dim])
        up = [(i, (i + 1) % size) for i in range(size - 1)]
        down = [(j, i) for i, j in up]
        last = lax.slice_in_dim(value, length - width, length, axis=dim)
        leading = lax.slice_in_dim(value, 0, width, axis=dim)
        before = lax.ppermute(last, axis, up)
        after = lax.ppermute(leading, axis, down)
        value = jnp.concatenate([before, value, after], axis=dim)
    return value


def tap_sum(padded, weight, row_count, col_count):
    channels = padded.shape[-1]
    summed = jnp.zeros((row_count * col_count, weight.shape[1]), jnp.float32)
    for frame_at in range(padded.shape[0]):
        for row_at in range(3):
            for col_at in range(3):
                tap_index = (frame_at * 3 + row_at) * 3 + col_at
                window = padded[
                    frame_at, row_at : row_at + row_count, col_at : col_at + col_count
                ].reshape(row_count * col_count, channels)
                summed = summed + jnp.dot(
                    window,
                    weight[tap_index * channels : (tap_index + 1) * channels],
                    preferred_element_type=jnp.float32,
                )
    return summed


def unfold_taps(padded, row_count, col_count):
    pieces = []
    for frame_at in range(padded.shape[0]):
        for row_at in range(3):
            for col_at in range(3):
                pieces.append(
                    padded[frame_at, row_at : row_at + row_count, col_at : col_at + col_count]
                )
    joined = jnp.concatenate(pieces, axis=-1)
    return joined.reshape(row_count * col_count, joined.shape[-1])


def token_routes(first, count, breadth, slot_cap, tile_rows, tile_cols, across, shard_count):
    offset = jnp.arange(slot_cap, dtype=jnp.int32)
    position = first[..., None] + offset
    live = offset < count[..., None]
    glob_row = position // breadth
    glob_col = position % breadth
    owner = jnp.where(live, glob_row // tile_rows * across + glob_col // tile_cols, shard_count)
    place = glob_row % tile_rows * tile_cols + glob_col % tile_cols
    return (owner, place)


def per_device(
    latent_shards,
    shard_starts,
    frame_dims,
    latent_cache,
    feature_cache,
    in_weight,
    in_bias,
    norm_gain,
    res_weight,
    res_bias,
    up_weight,
    up_bias,
):
    channels = in_bias.shape[0]
    latent_width = in_weight.shape[0] // 27
    out_width = up_bias.shape[0]
    tile_rows = feature_cache.shape[2]
    tile_cols = feature_cache.shape[3] // channels
    tile_cells = tile_rows * tile_cols
    across = lax.axis_size("tx")
    down_count = lax.axis_size("ty")
    shard_count = down_count * across
    row_index = lax.axis_index("ty")
    col_index = lax.axis_index("tx")
    myself = row_index * across + col_index
    height = frame_dims[0, 0]
    breadth = frame_dims[0, 1]
    starts = shard_starts[0]
    slot_cap = latent_shards.shape[1] // latent_width
    everything = lax.all_gather(latent_shards, ("ty", "tx"), axis=1, tiled=True).reshape(
        shard_count * slot_cap, latent_width
    )
    owner, place = token_routes(
        starts[:-1],
        starts[1:] - starts[:-1],
        breadth,
        slot_cap,
        tile_rows,
        tile_cols,
        across,
        shard_count,
    )
    target = jnp.where(owner == myself, place, tile_cells).reshape(-1)
    current = (
        jnp.zeros((tile_cells, latent_width), jnp.bfloat16).at[target].set(everything, mode="drop")
    )
    ycoord = row_index * tile_rows + jnp.arange(tile_rows, dtype=jnp.int32)
    xcoord = col_index * tile_cols + jnp.arange(tile_cols, dtype=jnp.int32)
    keep = ((ycoord[:, None] < height) & (xcoord[None, :] < breadth)).astype(jnp.float32)
    keep_low = keep.astype(jnp.bfloat16)[None, :, :, None]
    keep_flat = keep.reshape(-1, 1)
    lat_stack = (
        jnp.concatenate(
            [
                latent_cache[0].reshape(2, tile_rows, tile_cols, latent_width),
                current.reshape(1, tile_rows, tile_cols, latent_width),
            ],
            0,
        )
        * keep_low
    )
    lat_padded = padded_2(lat_stack, (("ty", 1), ("tx", 2)), 1)
    unfolded = unfold_taps(lat_padded, tile_rows, tile_cols)
    first_out = (jnp.dot(unfolded, in_weight, preferred_element_type=jnp.float32) + in_bias).astype(
        jnp.bfloat16
    )
    values = first_out.astype(jnp.float32)
    power = jnp.mean(values * values, axis=1, keepdims=True)
    normed = values * lax.rsqrt(power + EPS) * norm_gain
    hidden = (jax.nn.silu(normed) * keep_flat).astype(jnp.bfloat16)
    feat_stack = jnp.concatenate(
        [
            feature_cache[0].reshape(2, tile_rows, tile_cols, channels) * keep_low,
            hidden.reshape(1, tile_rows, tile_cols, channels),
        ],
        0,
    )
    feat_padded = padded_2(feat_stack, (("ty", 1), ("tx", 2)), 1)
    branch = tap_sum(feat_padded, res_weight, tile_rows, tile_cols)
    mixed = (
        ((values + branch + res_bias) * keep_flat)
        .astype(jnp.bfloat16)
        .reshape(tile_rows, tile_cols, channels)
    )
    low_padded = padded_2(mixed, (("ty", 0), ("tx", 1)), 1)
    grown_padded = jnp.repeat(jnp.repeat(low_padded, 2, axis=0), 2, axis=1)[1:-1, 1:-1]
    result = tap_sum(grown_padded[None], up_weight, 2 * tile_rows, 2 * tile_cols) + up_bias
    keep_high = jnp.repeat(jnp.repeat(keep, 2, axis=0), 2, axis=1).reshape(-1, 1)
    return (
        (result * keep_high)
        .astype(jnp.bfloat16)
        .reshape(1, 2 * tile_rows, 2 * tile_cols * out_width)
    )


def solution(mesh):
    return jax.shard_map(
        per_device,
        mesh=mesh,
        in_specs=(
            P("vid", ("ty", "tx")),
            P("vid", None),
            P("vid", None),
            P("vid", None, "ty", "tx"),
            P("vid", None, "ty", "tx"),
            P(),
            P(),
            P(),
            P(),
            P(),
            P(),
            P(),
        ),
        out_specs=P("vid", "ty", "tx"),
        check_vma=False,
    )
```

profile of v0, /device:TPU:1, one launch (start us, length us, event | category | flops | bytes accessed | tf_op | source)
XLA Modules:
  0.0 160.1 jit_solution(8422800603614920463)
XLA Ops:
  7.5 11.2 %all_gather.3 = bf16[1,99328]{1,0:T(2,128)(2,1)S(1)} all-gather(bf16[1,12416]{1,0:T(2,128)(2,1)} %param.12), channel_id=1, replica_groups=mesh['vid'=4,'ty'=2,'tx'=4] {'ty','tx'}, dimensions={1}, use_global_device_ids=true | all-gather | bytes 223488 | tf_op jit(solution)/shard_map/all_gather | solution.py:93
  23.1 24.5 %scatter_custom_fusion = bf16[512,16]{1,0:T(8,128)(2,1)S(1)} fusion(s32[6208]{0:T(1024)S(1)} %fusion.97, bf16[6208,16]{1,0:T(8,128)(2,1)S(1)} %reshape.439, bf16[]{:T(256)} %constant.70.clone.1), kind=kCustom, calls=%fused_computation.159 | custom fusion | bytes 16386 | tf_op jit(solution)/shard_map/scatter | solution.py:108
  47.8 2.9 %collective-permute-start = (bf16[3,1,32,16]{3,2,1,0:T(8,128)(2,1)S(1)}, bf16[3,1,32,16]{3,2,1,0:T(8,128)(2,1)S(1)}, u32[]{:S(2)}, u32[]{:S(2)}) collective-permute-start(bf16[3,1,32,16]{3,2,1,0:T(8,128)(2,1)S(1)} %get-tuple-element.84), channel_id=1, source_target_pairs={{0,4},{1,5},{2,6},{3,7},{8,12},{9,13},{10,14},{11,15},{16,20},{17,... | collective-permute-start | bytes 9224 | tf_op jit(solution)/shard_map/ppermute | solution.py:16
  52.3 1.4 fusion.72
  53.7 1.5 collective-permute-done.1
  56.2 3.5 %collective-permute-start.3 = (bf16[3,18,1,16]{3,2,1,0:T(2,128)(2,1)}, bf16[3,18,1,16]{3,2,1,0:T(2,128)(2,1)}, u32[]{:S(2)}, u32[]{:S(2)}) collective-permute-start(bf16[3,18,1,16]{3,2,1,0:T(2,128)(2,1)} %get-tuple-element.68), channel_id=1, source_target_pairs={{1,0},{2,1},{3,2},{5,4},{6,5},{7,6},{9,8},{10,9},{11,10},{13,12},{... | collective-permute-start | bytes 5192 | tf_op jit(solution)/shard_map/ppermute | solution.py:17
  59.7 2.5 %collective-permute-start.2 = (bf16[3,18,1,16]{3,2,1,0:T(2,128)(2,1)}, bf16[3,18,1,16]{3,2,1,0:T(2,128)(2,1)}, u32[]{:S(2)}, u32[]{:S(2)}) collective-permute-start(bf16[3,18,1,16]{3,2,1,0:T(2,128)(2,1)} %get-tuple-element.69), channel_id=1, source_target_pairs={{0,1},{1,2},{2,3},{4,5},{5,6},{6,7},{8,9},{9,10},{10,11},{12,13},{... | collective-permute-start | bytes 5192 | tf_op jit(solution)/shard_map/ppermute | solution.py:16
  63.0 1.6 copy.41
  88.7 1.7 %multiply_reduce_fusion = (f32[512]{0:T(512)S(1)}, f32[512,384]{1,0:T(8,128)S(1)}) fusion(f32[384]{0:T(512)S(1)} %copy-done.16, bf16[512,432]{0,1:T(8,128)(2,1)} %constant_dynamic-update-slice_fusion, bf16[432,384]{1,0:T(8,128)(2,1)S(1)} %copy-done), kind=kOutput, calls=%fused_computation.50 | convolution fusion | flops 170851840 | bytes 1564160 | tf_op jit(solution)/shard_map/dot_general | solution.py:127
  90.8 2.3 %collective-permute-start.4 = (bf16[3,1,32,384]{3,2,1,0:T(8,128)(2,1)S(1)}, bf16[3,1,32,384]{3,2,1,0:T(8,128)(2,1)S(1)}, u32[]{:S(2)}, u32[]{:S(2)}) collective-permute-start(bf16[3,1,32,384]{3,2,1,0:T(8,128)(2,1)S(1)} %get-tuple-element.45), channel_id=1, source_target_pairs={{0,4},{1,5},{2,6},{3,7},{8,12},{9,13},{10,14},{11,15},{16,20},{17,... | collective-permute-start | bytes 221192 | tf_op jit(solution)/shard_map/ppermute | solution.py:16
  95.7 2.9 %collective-permute-done.5 = bf16[3,1,32,384]{3,2,1,0:T(8,128)(2,1)S(1)} collective-permute-done((bf16[3,1,32,384]{3,2,1,0:T(8,128)(2,1)S(1)}, bf16[3,1,32,384]{3,2,1,0:T(8,128)(2,1)S(1)}, u32[]{:S(2)}, u32[]{:S(2)}) %collective-permute-start.5) | collective-permute-done | bytes 73760 | tf_op jit(solution)/shard_map/ppermute | solution.py:17
  100.5 3.3 %collective-permute-start.6 = (bf16[3,18,1,384]{3,2,1,0:T(2,128)(2,1)S(1)}, bf16[3,18,1,384]{3,2,1,0:T(2,128)(2,1)S(1)}, u32[]{:S(2)}, u32[]{:S(2)}) collective-permute-start(bf16[3,18,1,384]{3,2,1,0:T(2,128)(2,1)S(1)} %get-tuple-element.34), channel_id=1, source_target_pairs={{0,1},{1,2},{2,3},{4,5},{5,6},{6,7},{8,9},{9,10},{10,11},{12,13},{... | collective-permute-start | bytes 124424 | tf_op jit(solution)/shard_map/ppermute | solution.py:16
  103.8 2.1 %collective-permute-start.7 = (bf16[3,18,1,384]{3,2,1,0:T(2,128)(2,1)S(1)}, bf16[3,18,1,384]{3,2,1,0:T(2,128)(2,1)S(1)}, u32[]{:S(2)}, u32[]{:S(2)}) collective-permute-start(bf16[3,18,1,384]{3,2,1,0:T(2,128)(2,1)S(1)} %get-tuple-element.35), channel_id=1, source_target_pairs={{1,0},{2,1},{3,2},{5,4},{6,5},{7,6},{9,8},{10,9},{11,10},{13,12},{... | collective-permute-start | bytes 124424 | tf_op jit(solution)/shard_map/ppermute | solution.py:17
  110.3 1.9 %maximum_maximum_fusion = (bf16[3,18,33,384]{3,2,1,0:T(8,128)(2,1)S(1)}, bf16[3,18,33,384]{3,2,1,0:T(8,128)(2,1)S(1)}) fusion(bf16[3,1,32,384]{3,2,1,0:T(8,128)(2,1)S(1)} %collective-permute-done.5, bf16[1,16,32,384]{3,2,1,0:T(8,128)(2,1)S(1)} %bitcast.185, bf16[2,16,32,384]{3,2,1,0:T(8,128)(2,1)S(1)} %bitcast_multiply_fusion, ...), kind=kLoop, calls=%fused_computation.13 | loop fusion | flops 13685760 | bytes 4147200 | tf_op jit(solution)/shard_map/concatenate | solution.py:18
  112.2 2.0 %fusion.101 = (bf16[1,16,32,384]{3,2,1,0:T(8,128)(2,1)}, bf16[1,16,32,384]{3,2,1,0:T(8,128)(2,1)}, bf16[1,16,32,384]{3,2,1,0:T(8,128)(2,1)S(1)}, bf16[1,16,32,38...) fusion(bf16[3,18,33,384]{3,2,1,0:T(8,128)(2,1)S(1)} %get-tuple-, ...), kind=kLoop, calls=%fused_computation.218 | loop fusion | bytes 14155776 | tf_op jit(solution)/shard_map/slice | solution.py:29
  123.3 1.4 collective-permute-start.8
  126.1 3.3 %collective-permute-done.9 = bf16[1,32,384]{2,1,0:T(8,128)(2,1)S(1)} collective-permute-done((bf16[1,32,384]{2,1,0:T(8,128)(2,1)S(1)}, bf16[1,32,384]{2,1,0:T(8,128)(2,1)S(1)}, u32[]{:S(2)}, u32[]{:S(2)}) %collective-permute-start.9) | collective-permute-done | bytes 24608 | tf_op jit(solution)/shard_map/ppermute | solution.py:17
  129.4 5.1 %collective-permute-start.10 = (bf16[18,1,384]{2,1,0:T(2,128)(2,1)S(1)}, bf16[18,1,384]{2,1,0:T(2,128)(2,1)S(1)}, u32[]{:S(2)}, u32[]{:S(2)}) collective-permute-start(bf16[18,1,384]{2,1,0:T(2,128)(2,1)S(1)} %get-tuple-element.48), channel_id=1, source_target_pairs={{0,1},{1,2},{2,3},{4,5},{5,6},{6,7},{8,9},{9,10},{10,11},{12,13},{... | collective-permute-start | bytes 41480 | tf_op jit(solution)/shard_map/ppermute | solution.py:16
  134.5 2.2 %collective-permute-start.11 = (bf16[18,1,384]{2,1,0:T(2,128)(2,1)S(1)}, bf16[18,1,384]{2,1,0:T(2,128)(2,1)S(1)}, u32[]{:S(2)}, u32[]{:S(2)}) collective-permute-start(bf16[18,1,384]{2,1,0:T(2,128)(2,1)S(1)} %get-tuple-element.49), channel_id=1, source_target_pairs={{1,0},{2,1},{3,2},{5,4},{6,5},{7,6},{9,8},{10,9},{11,10},{13,12},{... | collective-permute-start | bytes 41480 | tf_op jit(solution)/shard_map/ppermute | solution.py:17
  137.2 2.5 %collective-permute-done.11 = bf16[18,1,384]{2,1,0:T(2,128)(2,1)S(1)} collective-permute-done((bf16[18,1,384]{2,1,0:T(2,128)(2,1)S(1)}, bf16[18,1,384]{2,1,0:T(2,128)(2,1)S(1)}, u32[]{:S(2)}, u32[]{:S(2)}) %collective-permute-start.11) | collective-permute-done | bytes 13856 | tf_op jit(solution)/shard_map/ppermute | solution.py:17
  140.0 2.2 %broadcast_in_dim.42 = bf16[36,34,2,384]{3,2,1,0:T(2,128)(2,1)} broadcast(bf16[36,34,384]{2,1,0:T(8,128)(2,1)S(1)} %bitcast.197), dimensions={0,1,3} | broadcast | bytes 2820096 | tf_op jit(solution)/shard_map/broadcast_in_dim | solution.py:149
  142.2 4.2 %reshape.431 = bf16[36,68,384]{2,1,0:T(8,128)(2,1)S(1)} reshape(bf16[36,34,2,384]{3,2,1,0:T(2,128)(2,1)} %broadcast_in_dim.42) | data formatting | bytes 3760128 | tf_op jit(solution)/shard_map/reshape | solution.py:149
  147.3 3.6 %fusion.100 = (bf16[1,32,64,384]{3,2,1,0:T(8,128)(2,1)S(1)}, bf16[1,32,64,384]{3,2,1,0:T(8,128)(2,1)S(1)}, bf16[1,32,64,384]{3,2,1,0:T(8,128)(2,1)S(1)}, bf16[1,...) fusion(bf16[1,34,66,384]{3,2,1,0:T(8,128)(2,1)S(1)} %slice_bitc, ...), kind=kLoop, calls=%fused_computation.217 | loop fusion | bytes 28311552 | tf_op jit(solution)/shard_map/slice | solution.py:29
  158.0 2.1 %reshape.433 = bf16[1,32,12288]{2,1,0:T(8,128)(2,1)} reshape(bf16[2048,192]{1,0:T(8,128)(2,1)S(1)} %copy.50) | data formatting | bytes 1572864 | tf_op jit(solution)/shard_map/reshape | solution.py:155
  (201 shorter events, 65.5 us)
Async XLA Ops:
  0.0 88.7 %copy-start = (bf16[432,384]{1,0:T(8,128)(2,1)S(1)}, bf16[432,384]{1,0:T(8,128)(2,1)}, u32[]{:S(2)}) copy-start(bf16[432,384]{1,0:T(8,128)(2,1)} %param.17) | copy-start | bytes 995332
  0.0 21.6 %copy-start.12 = (bf16[1,2,16,512]{3,2,1,0:T(8,128)(2,1)S(1)}, bf16[1,2,16,512]{3,2,1,0:T(8,128)(2,1)}, u32[]{:S(2)}) copy-start(bf16[1,2,16,512]{3,2,1,0:T(8,128)(2,1)} %param.15) | copy-start | bytes 98308
  20.0 32.0 %copy-start.9 = (bf16[1,2,16,12288]{3,2,1,0:T(8,128)(2,1)S(1)}, bf16[1,2,16,12288]{3,2,1,0:T(8,128)(2,1)}, u32[]{:S(2)}) copy-start(bf16[1,2,16,12288]{3,2,1,0:T(8,128)(2,1)} %param.16) | copy-start | bytes 2359300
  47.8 6.0 %collective-permute-start = (bf16[3,1,32,16]{3,2,1,0:T(8,128)(2,1)S(1)}, bf16[3,1,32,16]{3,2,1,0:T(8,128)(2,1)S(1)}, u32[]{:S(2)}, u32[]{:S(2)}) collective-permute-start(bf16[3,1,32,16]{3,2,1,0:T(8,128)(2,1)S(1)} %get-tuple-element.84), channel_id=1, source_target_pairs={{0,4},{1,5},{2,6},{3,7},{8,12},{9,13},{10,14},{11,15},{16,20},{17,... | collective-permute-start | bytes 9224 | tf_op jit(solution)/shard_map/ppermute | solution.py:16
  50.6 4.6 %collective-permute-start.1 = (bf16[3,1,32,16]{3,2,1,0:T(8,128)(2,1)S(1)}, bf16[3,1,32,16]{3,2,1,0:T(8,128)(2,1)S(1)}, u32[]{:S(2)}, u32[]{:S(2)}) collective-permute-start(bf16[3,1,32,16]{3,2,1,0:T(8,128)(2,1)S(1)} %get-tuple-element.85), channel_id=1, source_target_pairs={{4,0},{5,1},{6,2},{7,3},{12,8},{13,9},{14,10},{15,11},{20,16},{21,... | collective-permute-start | bytes 9224 | tf_op jit(solution)/shard_map/ppermute | solution.py:17
  56.2 9.9 %collective-permute-start.3 = (bf16[3,18,1,16]{3,2,1,0:T(2,128)(2,1)}, bf16[3,18,1,16]{3,2,1,0:T(2,128)(2,1)}, u32[]{:S(2)}, u32[]{:S(2)}) collective-permute-start(bf16[3,18,1,16]{3,2,1,0:T(2,128)(2,1)} %get-tuple-element.68), channel_id=1, source_target_pairs={{1,0},{2,1},{3,2},{5,4},{6,5},{7,6},{9,8},{10,9},{11,10},{13,12},{... | collective-permute-start | bytes 5192 | tf_op jit(solution)/shard_map/ppermute | solution.py:17
  59.7 8.7 %collective-permute-start.2 = (bf16[3,18,1,16]{3,2,1,0:T(2,128)(2,1)}, bf16[3,18,1,16]{3,2,1,0:T(2,128)(2,1)}, u32[]{:S(2)}, u32[]{:S(2)}) collective-permute-start(bf16[3,18,1,16]{3,2,1,0:T(2,128)(2,1)} %get-tuple-element.69), channel_id=1, source_target_pairs={{0,1},{1,2},{2,3},{4,5},{5,6},{6,7},{8,9},{9,10},{10,11},{12,13},{... | collective-permute-start | bytes 5192 | tf_op jit(solution)/shard_map/ppermute | solution.py:16
  70.8 2.2 %copy-start.10 = (bf16[512,16]{0,1:T(8,128)(2,1)S(1)}, bf16[512,16]{0,1:T(8,128)(2,1)}, u32[]{:S(2)}) copy-start(bf16[512,16]{0,1:T(8,128)(2,1)} %copy.41) | copy-start | bytes 49156
  70.8 2.8 %copy-start.11 = (bf16[512,16]{0,1:T(8,128)(2,1)S(1)}, bf16[512,16]{0,1:T(8,128)(2,1)}, u32[]{:S(2)}) copy-start(bf16[512,16]{0,1:T(8,128)(2,1)} %concatenate.149) | copy-start | bytes 49156
  71.3 17.4 %copy-start.16 = (f32[384]{0:T(512)S(1)}, f32[384]{0:T(512)}, u32[]{:S(2)}) copy-start(f32[384]{0:T(512)} %param.18) | copy-start | bytes 4612
  72.6 17.8 %copy-start.13 = (f32[384]{0:T(512)S(1)}, f32[384]{0:T(512)}, u32[]{:S(2)}) copy-start(f32[384]{0:T(512)} %param.19) | copy-start | bytes 4612
  88.7 18.6 %slice-start = ((s8[7962624]{0:T(1024)(128)(4,1)}), s8[4194304]{0:T(1024)(128)(4,1)S(1)}, s32[]{:S(2)}) async-start(s8[7962624]{0:T(1024)(128)(4,1)} %bitcast.186), calls=%async_computation | async-start | bytes 8388608
  90.8 4.9 %collective-permute-start.4 = (bf16[3,1,32,384]{3,2,1,0:T(8,128)(2,1)S(1)}, bf16[3,1,32,384]{3,2,1,0:T(8,128)(2,1)S(1)}, u32[]{:S(2)}, u32[]{:S(2)}) collective-permute-start(bf16[3,1,32,384]{3,2,1,0:T(8,128)(2,1)S(1)} %get-tuple-element.45), channel_id=1, source_target_pairs={{0,4},{1,5},{2,6},{3,7},{8,12},{9,13},{10,14},{11,15},{16,20},{17,... | collective-permute-start | bytes 221192 | tf_op jit(solution)/shard_map/ppermute | solution.py:16
  93.1 5.6 %collective-permute-start.5 = (bf16[3,1,32,384]{3,2,1,0:T(8,128)(2,1)S(1)}, bf16[3,1,32,384]{3,2,1,0:T(8,128)(2,1)S(1)}, u32[]{:S(2)}, u32[]{:S(2)}) collective-permute-start(bf16[3,1,32,384]{3,2,1,0:T(8,128)(2,1)S(1)} %get-tuple-element.46), channel_id=1, source_target_pairs={{4,0},{5,1},{6,2},{7,3},{12,8},{13,9},{14,10},{15,11},{20,16},{21,... | collective-permute-start | bytes 221192 | tf_op jit(solution)/shard_map/ppermute | solution.py:17
  95.7 11.6 %slice-start.1 = ((s8[7962624]{0:T(1024)(128)(4,1)}), s8[3768320]{0:T(1024)(128)(4,1)S(1)}, s32[]{:S(2)}) async-start(s8[7962624]{0:T(1024)(128)(4,1)} %bitcast.186), calls=%async_computation.1 | async-start | bytes 7536640
  100.5 9.7 %collective-permute-start.6 = (bf16[3,18,1,384]{3,2,1,0:T(2,128)(2,1)S(1)}, bf16[3,18,1,384]{3,2,1,0:T(2,128)(2,1)S(1)}, u32[]{:S(2)}, u32[]{:S(2)}) collective-permute-start(bf16[3,18,1,384]{3,2,1,0:T(2,128)(2,1)S(1)} %get-tuple-element.34), channel_id=1, source_target_pairs={{0,1},{1,2},{2,3},{4,5},{5,6},{6,7},{8,9},{9,10},{10,11},{12,13},{... | collective-permute-start | bytes 124424 | tf_op jit(solution)/shard_map/ppermute | solution.py:16
  103.8 6.4 %collective-permute-start.7 = (bf16[3,18,1,384]{3,2,1,0:T(2,128)(2,1)S(1)}, bf16[3,18,1,384]{3,2,1,0:T(2,128)(2,1)S(1)}, u32[]{:S(2)}, u32[]{:S(2)}) collective-permute-start(bf16[3,18,1,384]{3,2,1,0:T(2,128)(2,1)S(1)} %get-tuple-element.35), channel_id=1, source_target_pairs={{1,0},{2,1},{3,2},{5,4},{6,5},{7,6},{9,8},{10,9},{11,10},{13,12},{... | collective-permute-start | bytes 124424 | tf_op jit(solution)/shard_map/ppermute | solution.py:17
  121.5 1.2 copy-start.3
  123.3 2.7 %collective-permute-start.8 = (bf16[1,32,384]{2,1,0:T(8,128)(2,1)S(1)}, bf16[1,32,384]{2,1,0:T(8,128)(2,1)S(1)}, u32[]{:S(2)}, u32[]{:S(2)}) collective-permute-start(bf16[1,32,384]{2,1,0:T(8,128)(2,1)S(1)} %get-tuple-element.76), channel_id=1, source_target_pairs={{0,4},{1,5},{2,6},{3,7},{8,12},{9,13},{10,14},{11,15},{16,20},{17,... | collective-permute-start | bytes 73736 | tf_op jit(solution)/shard_map/ppermute | solution.py:16
  124.8 4.6 %collective-permute-start.9 = (bf16[1,32,384]{2,1,0:T(8,128)(2,1)S(1)}, bf16[1,32,384]{2,1,0:T(8,128)(2,1)S(1)}, u32[]{:S(2)}, u32[]{:S(2)}) collective-permute-start(bf16[1,32,384]{2,1,0:T(8,128)(2,1)S(1)} %get-tuple-element.77), channel_id=1, source_target_pairs={{4,0},{5,1},{6,2},{7,3},{12,8},{13,9},{14,10},{15,11},{20,16},{21,... | collective-permute-start | bytes 73736 | tf_op jit(solution)/shard_map/ppermute | solution.py:17
  129.4 7.8 %collective-permute-start.10 = (bf16[18,1,384]{2,1,0:T(2,128)(2,1)S(1)}, bf16[18,1,384]{2,1,0:T(2,128)(2,1)S(1)}, u32[]{:S(2)}, u32[]{:S(2)}) collective-permute-start(bf16[18,1,384]{2,1,0:T(2,128)(2,1)S(1)} %get-tuple-element.48), channel_id=1, source_target_pairs={{0,1},{1,2},{2,3},{4,5},{5,6},{6,7},{8,9},{9,10},{10,11},{12,13},{... | collective-permute-start | bytes 41480 | tf_op jit(solution)/shard_map/ppermute | solution.py:16
  134.5 5.2 %collective-permute-start.11 = (bf16[18,1,384]{2,1,0:T(2,128)(2,1)S(1)}, bf16[18,1,384]{2,1,0:T(2,128)(2,1)S(1)}, u32[]{:S(2)}, u32[]{:S(2)}) collective-permute-start(bf16[18,1,384]{2,1,0:T(2,128)(2,1)S(1)} %get-tuple-element.49), channel_id=1, source_target_pairs={{1,0},{2,1},{3,2},{5,4},{6,5},{7,6},{9,8},{10,9},{11,10},{13,12},{... | collective-permute-start | bytes 41480 | tf_op jit(solution)/shard_map/ppermute | solution.py:17
  147.3 3.6 %copy-start.8 = (bf16[3456,192]{0,1:T(8,128)(2,1)S(1)}, bf16[3456,192]{0,1:T(8,128)(2,1)}, u32[]{:S(2)}) copy-start(bf16[3456,192]{0,1:T(8,128)(2,1)} %param.22) | copy-start | bytes 3981316
  156.8 3.3 %copy-start.1 = (bf16[432,384]{1,0:T(8,128)(2,1)S(1)}, bf16[432,384]{1,0:T(8,128)(2,1)}, u32[]{:S(2)}) copy-start(bf16[432,384]{1,0:T(8,128)(2,1)} %param.17) | copy-start | bytes 995332
  (7 other events, 7.2 us)
where the time goes:
time: 161 us; the launch traced here: 160 us
  local copies, waits for them, and re-layouts  71.1 us (44%)
  starting transfers between devices  29.1 us (18%)
  matrix products  24.5 us (15%)
  blocking collectives  11.2 us (7%)
  other arithmetic  11.1 us (7%)
  waiting for transfers between devices  10.2 us (6%)
  between operations  2.86 us (2%)
    scatter x1, local copies, waits for them, and re-layouts, per_device(): jnp.zeros((tile_cells, latent_width), jnp.bfloat16).at[target]  24.5 us
    dot_general x36, matrix products, tap_sum(): jnp.dot(window, weight[tap_index * channels:(tap_index + 1) * channels],...  22.8 us
    ppermute x6, starting transfers between devices, padded_2(): before = lax.ppermute(last, axis, up)  17.4 us
    unnamed x65, local copies, waits for them, and re-layouts  16.8 us
    ppermute x6, starting transfers between devices, padded_2(): after = lax.ppermute(leading, axis, down)  11.7 us
    all_gather x1, blocking collectives, per_device(): lax.all_gather(latent_shards, ('ty', 'tx'), axis=1, tiled=True)  11.2 us
    ppermute x6, waiting for transfers between devices, padded_2(): after = lax.ppermute(leading, axis, down)  10.2 us
    concatenate x28, local copies, waits for them, and re-layouts, unfold_taps(): joined = jnp.concatenate(pieces, axis=-1)  6.48 us
  transfers between devices with their start and end apart: 12, of which 4 were waited for; matrix products, arithmetic and copies ran while one was open for 9% of the time, Pallas kernels for 0%

commit v1 on v0

--- a/solution.py
+++ b/solution.py
@@ -90,9 +90,31 @@
     breadth = frame_dims[0, 1]
     starts = shard_starts[0]
     slot_cap = latent_shards.shape[1] // latent_width
-    everything = lax.all_gather(latent_shards, ("ty", "tx"), axis=1, tiled=True).reshape(
-        shard_count * slot_cap, latent_width
-    )
+
+    def launch_scenes_up(block_in, along_dim):
+        a_name = ("ty", "tx")
+        earlier, x_next, reply = (
+            lax.axis_size(a_name),
+            lax.axis_index(a_name),
+            block_in.shape[along_dim],
+        )
+        local_part, k_now = (block_in, 1)
+        while k_now < earlier:
+            local_part = jnp.concatenate(
+                [
+                    local_part,
+                    lax.ppermute(
+                        local_part,
+                        axis_name=a_name,
+                        perm=list(map(lambda ii: (ii, (ii - k_now) % earlier), range(earlier))),
+                    ),
+                ],
+                along_dim,
+            )
+            k_now = 2 * k_now
+        return jnp.roll(local_part, x_next * reply, along_dim)
+
+    everything = launch_scenes_up(latent_shards, 1).reshape(shard_count * slot_cap, latent_width)
     owner, place = token_routes(
         starts[:-1],
         starts[1:] - starts[:-1],

time: 161 us -> 150 us (0.932)
  blocking collectives: 11.2 us -> 0 us
  local copies, waits for them, and re-layouts: 71.1 us -> 61.3 us
  starting transfers between devices: 29.1 us -> 37 us
  waiting for transfers between devices: 10.2 us -> 15 us
    all_gather x1 -> x0, blocking collectives: 11.2 us -> none  [per_device(): lax.all_gather(latent_shards, ('ty', 'tx'), axis=1, tiled=True)]
    unnamed x65 -> x78, local copies, waits for them, and re-layouts: 16.8 us -> 9.48 us
    ppermute x0 -> x3, waiting for transfers between devices: none -> 4.92 us  [launch_scenes_up(): lax.ppermute(local_part, axis_name=a_name, perm=list(map(lambda ii: (ii,...]
    ppermute x0 -> x3, starting transfers between devices: none -> 4.14 us  [launch_scenes_up(): lax.ppermute(local_part, axis_name=a_name, perm=list(map(lambda ii: (ii,...]
    concatenate x28, local copies, waits for them, and re-layouts: 6.48 us -> 2.88 us  [unfold_taps(): joined = jnp.concatenate(pieces, axis=-1)]
    ppermute x6, starting transfers between devices: 11.7 us -> 14.5 us  [padded_2(): after = lax.ppermute(leading, axis, down)]
    dynamic_slice x0 -> x1, local copies, waits for them, and re-layouts: none -> 2.11 us  [launch_scenes_up(): return jnp.roll(local_part, x_next * reply, along_dim)]
    slice x3 -> x4, local copies, waits for them, and re-layouts: 5.63 us -> 5.81 us  [tap_sum(): padded[frame_at, row_at:row_at + row_count, col_at:col_at + col_count]]
  transfers between devices with their start and end apart: 12 -> 15, of which waited for: 4 -> 6; matrix products, arithmetic and copies ran while one was open for 9% -> 14% of each run, Pallas kernels for 0% -> 0%
where the time goes in v1:
time: 150 us; the launch traced here: 149 us
  local copies, waits for them, and re-layouts  61.3 us (41%)
  starting transfers between devices  37 us (25%)
  matrix products  23.4 us (16%)
  waiting for transfers between devices  15 us (10%)
  other arithmetic  9.59 us (6%)
  between operations  3.23 us (2%)
    scatter x1, local copies, waits for them, and re-layouts, per_device(): jnp.zeros((tile_cells, latent_width), jnp.bfloat16).at[target]  24.5 us
    dot_general x36, matrix products, tap_sum(): jnp.dot(window, weight[tap_index * channels:(tap_index + 1) * channels],...  22.8 us
    ppermute x6, starting transfers between devices, padded_2(): before = lax.ppermute(last, axis, up)  18.4 us
    ppermute x6, starting transfers between devices, padded_2(): after = lax.ppermute(leading, axis, down)  14.5 us
    ppermute x6, waiting for transfers between devices, padded_2(): after = lax.ppermute(leading, axis, down)  10 us
    unnamed x78, local copies, waits for them, and re-layouts  9.48 us
    slice x4, local copies, waits for them, and re-layouts, tap_sum(): padded[frame_at, row_at:row_at + row_count, col_at:col_at + col_count]  5.81 us
    ppermute x3, waiting for transfers between devices, launch_scenes_up(): lax.ppermute(local_part, axis_name=a_name, perm=list(map(lambda ii: (ii,...  4.92 us
  transfers between devices with their start and end apart: 15, of which 6 were waited for; matrix products, arithmetic and copies ran while one was open for 14% of the time, Pallas kernels for 0%

profile of v1, /device:TPU:1, one launch (start us, length us, event | category | flops | bytes accessed | tf_op | source)
XLA Modules:
  0.0 149.5 jit_solution(12289595065302862377)
XLA Ops:
  0.1 1.5 %constant_dynamic-update-slice_fusion.7 = bf16[1,198656]{1,0:T(2,128)(2,1)} fusion(bf16[1,12416]{1,0:T(2,128)(2,1)} %param.12), kind=kLoop, calls=%fused_computation.149 | loop fusion | bytes 74496
  13.0 3.6 %collective-permute-start.1 = (bf16[1,24832]{1,0:T(2,128)(2,1)S(1)}, bf16[1,24832]{1,0:T(2,128)(2,1)S(1)}, u32[]{:S(2)}, u32[]{:S(2)}) collective-permute-start(bf16[1,24832]{1,0:T(2,128)(2,1)S(1)} %pad_maximum_fusion.18), channel_id=1, source_target_pairs={{0,6},{1,7},{2,0},{3,1},{4,2},{5,3},{6,4},{7,5},{8,14},{9,15},{10,... | collective-permute-start | bytes 149000 | tf_op jit(solution)/shard_map/ppermute | solution.py:106
  17.3 1.5 %collective-permute-done.1 = bf16[1,24832]{1,0:T(2,128)(2,1)S(1)} collective-permute-done((bf16[1,24832]{1,0:T(2,128)(2,1)S(1)}, bf16[1,24832]{1,0:T(2,128)(2,1)S(1)}, u32[]{:S(2)}, u32[]{:S(2)}) %collective-permute-start.1) | collective-permute-done | bytes 49696 | tf_op jit(solution)/shard_map/ppermute | solution.py:106
  20.2 3.4 %collective-permute-done.2 = bf16[1,49664]{1,0:T(2,128)(2,1)S(1)} collective-permute-done((bf16[1,49664]{1,0:T(2,128)(2,1)S(1)}, bf16[1,49664]{1,0:T(2,128)(2,1)S(1)}, u32[]{:S(2)}, u32[]{:S(2)}) %collective-permute-start.2) | collective-permute-done | bytes 99360 | tf_op jit(solution)/shard_map/ppermute | solution.py:106
  27.5 2.1 %dynamic-slice_reduce_fusion = bf16[99328]{0:T(1024)(128)(2,1)S(1)} fusion(bf16[1,198656]{1,0:T(2,128)(2,1)} %constant_dynamic-update-slice_fusion, s32[]{:T(128)S(6)} %select_n.135), kind=kLoop, calls=%fused_computation.53 | loop fusion | bytes 397316 | tf_op jit(solution)/shard_map/jit(_roll_dynamic)/dynamic_slice | solution.py:115
  30.6 24.5 %scatter_custom_fusion = bf16[512,16]{1,0:T(8,128)(2,1)S(1)} fusion(s32[6208]{0:T(1024)S(1)} %fusion.97, bf16[6208,16]{1,0:T(8,128)(2,1)S(1)} %reshape.439, bf16[]{:T(256)} %constant.87.clone.1), kind=kCustom, calls=%fused_computation.197 | custom fusion | bytes 16386 | tf_op jit(solution)/shard_map/scatter | solution.py:130
  55.2 2.3 %collective-permute-start.3 = (bf16[3,1,32,16]{3,2,1,0:T(8,128)(2,1)S(1)}, bf16[3,1,32,16]{3,2,1,0:T(8,128)(2,1)S(1)}, u32[]{:S(2)}, u32[]{:S(2)}) collective-permute-start(bf16[3,1,32,16]{3,2,1,0:T(8,128)(2,1)S(1)} %get-tuple-element.84), channel_id=1, source_target_pairs={{0,4},{1,5},{2,6},{3,7},{8,12},{9,13},{10,14},{11,15},{16,20},{17,... | collective-permute-start | bytes 9224 | tf_op jit(solution)/shard_map/ppermute | solution.py:16
  60.3 1.8 %collective-permute-done.4 = bf16[3,1,32,16]{3,2,1,0:T(8,128)(2,1)S(1)} collective-permute-done((bf16[3,1,32,16]{3,2,1,0:T(8,128)(2,1)S(1)}, bf16[3,1,32,16]{3,2,1,0:T(8,128)(2,1)S(1)}, u32[]{:S(2)}, u32[]{:S(2)}) %collective-permute-start.4) | collective-permute-done | bytes 3104 | tf_op jit(solution)/shard_map/ppermute | solution.py:17
  62.3 6.5 %collective-permute-start.6 = (bf16[3,18,1,16]{3,2,1,0:T(2,128)(2,1)S(1)}, bf16[3,18,1,16]{3,2,1,0:T(2,128)(2,1)S(1)}, u32[]{:S(2)}, u32[]{:S(2)}) collective-permute-start(bf16[3,18,1,16]{3,2,1,0:T(2,128)(2,1)S(1)} %get-tuple-element.68), channel_id=1, source_target_pairs={{1,0},{2,1},{3,2},{5,4},{6,5},{7,6},{9,8},{10,9},{11,10},{13,12},{... | collective-permute-start | bytes 5192 | tf_op jit(solution)/shard_map/ppermute | solution.py:17
  69.2 4.6 %collective-permute-start.5 = (bf16[3,18,1,16]{3,2,1,0:T(2,128)(2,1)S(1)}, bf16[3,18,1,16]{3,2,1,0:T(2,128)(2,1)S(1)}, u32[]{:S(2)}, u32[]{:S(2)}) collective-permute-start(bf16[3,18,1,16]{3,2,1,0:T(2,128)(2,1)S(1)} %get-tuple-element.69), channel_id=1, source_target_pairs={{0,1},{1,2},{2,3},{4,5},{5,6},{6,7},{8,9},{9,10},{10,11},{12,13},{... | collective-permute-start | bytes 5192 | tf_op jit(solution)/shard_map/ppermute | solution.py:16
  80.6 1.5 collective-permute-start.7
  84.8 2.4 %collective-permute-done.8 = bf16[3,1,32,384]{3,2,1,0:T(8,128)(2,1)S(1)} collective-permute-done((bf16[3,1,32,384]{3,2,1,0:T(8,128)(2,1)S(1)}, bf16[3,1,32,384]{3,2,1,0:T(8,128)(2,1)S(1)}, u32[]{:S(2)}, u32[]{:S(2)}) %collective-permute-start.8) | collective-permute-done | bytes 73760 | tf_op jit(solution)/shard_map/ppermute | solution.py:17
  89.1 1.9 %collective-permute-start.10 = (bf16[3,18,1,384]{3,2,1,0:T(2,128)(2,1)S(1)}, bf16[3,18,1,384]{3,2,1,0:T(2,128)(2,1)S(1)}, u32[]{:S(2)}, u32[]{:S(2)}) collective-permute-start(bf16[3,18,1,384]{3,2,1,0:T(2,128)(2,1)S(1)} %get-tuple-element.35), channel_id=1, source_target_pairs={{1,0},{2,1},{3,2},{5,4},{6,5},{7,6},{9,8},{10,9},{11,10},{13,12},{... | collective-permute-start | bytes 124424 | tf_op jit(solution)/shard_map/ppermute | solution.py:17
  91.0 4.8 %collective-permute-start.9 = (bf16[3,18,1,384]{3,2,1,0:T(2,128)(2,1)S(1)}, bf16[3,18,1,384]{3,2,1,0:T(2,128)(2,1)S(1)}, u32[]{:S(2)}, u32[]{:S(2)}) collective-permute-start(bf16[3,18,1,384]{3,2,1,0:T(2,128)(2,1)S(1)} %get-tuple-element.34), channel_id=1, source_target_pairs={{0,1},{1,2},{2,3},{4,5},{5,6},{6,7},{8,9},{9,10},{10,11},{12,13},{... | collective-permute-start | bytes 124424 | tf_op jit(solution)/shard_map/ppermute | solution.py:16
  100.1 1.9 %maximum_maximum_fusion = (bf16[3,18,33,384]{3,2,1,0:T(8,128)(2,1)S(1)}, bf16[3,18,33,384]{3,2,1,0:T(8,128)(2,1)S(1)}) fusion(bf16[3,1,32,384]{3,2,1,0:T(8,128)(2,1)S(1)} %collective-permute-done.8, bf16[1,16,32,384]{3,2,1,0:T(8,128)(2,1)S(1)} %bitcast.186, bf16[2,16,32,384]{3,2,1,0:T(8,128)(2,1)S(1)} %copy-done.3, ...), kind=kLoop, calls=%fused_computation.13 | loop fusion | flops 13685760 | bytes 4147200 | tf_op jit(solution)/shard_map/concatenate | solution.py:18
  102.1 2.2 %fusion.101 = (bf16[1,16,32,384]{3,2,1,0:T(8,128)(2,1)}, bf16[1,16,32,384]{3,2,1,0:T(8,128)(2,1)}, bf16[1,16,32,384]{3,2,1,0:T(8,128)(2,1)S(1)}, bf16[1,16,32,38...) fusion(bf16[3,18,33,384]{3,2,1,0:T(8,128)(2,1)S(1)} %get-tuple-, ...), kind=kLoop, calls=%fused_computation.229 | loop fusion | bytes 14155776 | tf_op jit(solution)/shard_map/slice | solution.py:29
  116.7 3.3 %collective-permute-done.12 = bf16[1,32,384]{2,1,0:T(8,128)(2,1)S(1)} collective-permute-done((bf16[1,32,384]{2,1,0:T(8,128)(2,1)S(1)}, bf16[1,32,384]{2,1,0:T(8,128)(2,1)S(1)}, u32[]{:S(2)}, u32[]{:S(2)}) %collective-permute-start.12) | collective-permute-done | bytes 24608 | tf_op jit(solution)/shard_map/ppermute | solution.py:17
  120.0 3.8 %collective-permute-start.13 = (bf16[18,1,384]{2,1,0:T(2,128)(2,1)S(1)}, bf16[18,1,384]{2,1,0:T(2,128)(2,1)S(1)}, u32[]{:S(2)}, u32[]{:S(2)}) collective-permute-start(bf16[18,1,384]{2,1,0:T(2,128)(2,1)S(1)} %get-tuple-element.48), channel_id=1, source_target_pairs={{0,1},{1,2},{2,3},{4,5},{5,6},{6,7},{8,9},{9,10},{10,11},{12,13},{... | collective-permute-start | bytes 41480 | tf_op jit(solution)/shard_map/ppermute | solution.py:16
  123.8 2.1 %collective-permute-start.14 = (bf16[18,1,384]{2,1,0:T(2,128)(2,1)S(1)}, bf16[18,1,384]{2,1,0:T(2,128)(2,1)S(1)}, u32[]{:S(2)}, u32[]{:S(2)}) collective-permute-start(bf16[18,1,384]{2,1,0:T(2,128)(2,1)S(1)} %get-tuple-element.49), channel_id=1, source_target_pairs={{1,0},{2,1},{3,2},{5,4},{6,5},{7,6},{9,8},{10,9},{11,10},{13,12},{... | collective-permute-start | bytes 41480 | tf_op jit(solution)/shard_map/ppermute | solution.py:17
  126.5 2.5 %collective-permute-done.14 = bf16[18,1,384]{2,1,0:T(2,128)(2,1)S(1)} collective-permute-done((bf16[18,1,384]{2,1,0:T(2,128)(2,1)S(1)}, bf16[18,1,384]{2,1,0:T(2,128)(2,1)S(1)}, u32[]{:S(2)}, u32[]{:S(2)}) %collective-permute-start.14) | collective-permute-done | bytes 13856 | tf_op jit(solution)/shard_map/ppermute | solution.py:17
  129.4 2.3 %broadcast_in_dim.42 = bf16[36,34,2,384]{3,2,1,0:T(2,128)(2,1)} broadcast(bf16[36,34,384]{2,1,0:T(8,128)(2,1)S(1)} %bitcast.198), dimensions={0,1,3} | broadcast | bytes 2820096 | tf_op jit(solution)/shard_map/broadcast_in_dim | solution.py:171
  131.6 4.2 %reshape.431 = bf16[36,68,384]{2,1,0:T(8,128)(2,1)S(1)} reshape(bf16[36,34,2,384]{3,2,1,0:T(2,128)(2,1)} %broadcast_in_dim.42) | data formatting | bytes 3760128 | tf_op jit(solution)/shard_map/reshape | solution.py:171
  136.7 3.6 %fusion.100 = (bf16[1,32,64,384]{3,2,1,0:T(8,128)(2,1)S(1)}, bf16[1,32,64,384]{3,2,1,0:T(8,128)(2,1)S(1)}, bf16[1,32,64,384]{3,2,1,0:T(8,128)(2,1)S(1)}, bf16[1,...) fusion(bf16[1,34,66,384]{3,2,1,0:T(8,128)(2,1)S(1)} %slice_bitc, ...), kind=kLoop, calls=%fused_computation.228 | loop fusion | bytes 28311552 | tf_op jit(solution)/shard_map/slice | solution.py:29
  147.4 2.0 %reshape.433 = bf16[1,32,12288]{2,1,0:T(8,128)(2,1)} reshape(bf16[2048,192]{1,0:T(8,128)(2,1)S(1)} %copy.50) | data formatting | bytes 1572864 | tf_op jit(solution)/shard_map/reshape | solution.py:177
  (223 shorter events, 55.8 us)
Async XLA Ops:
  0.0 79.5 %copy-start = (bf16[432,384]{1,0:T(8,128)(2,1)S(1)}, bf16[432,384]{1,0:T(8,128)(2,1)}, u32[]{:S(2)}) copy-start(bf16[432,384]{1,0:T(8,128)(2,1)} %param.17) | copy-start | bytes 995332
  0.0 12.9 %collective-permute-start = (bf16[1,12416]{1,0:T(2,128)(2,1)}, bf16[1,12416]{1,0:T(2,128)(2,1)S(1)}, u32[]{:S(2)}, u32[]{:S(2)}) collective-permute-start(bf16[1,12416]{1,0:T(2,128)(2,1)} %param.12), channel_id=1, source_target_pairs={{0,7},{1,0},{2,1},{3,2},{4,3},{5,4},{6,5},{7,6},{8,15},{9,8},{10,9... | collective-permute-start | bytes 74504 | tf_op jit(solution)/shard_map/ppermute | solution.py:106
  9.8 2.8 %copy-start.14 = (bf16[1,2,16,512]{3,2,1,0:T(8,128)(2,1)S(1)}, bf16[1,2,16,512]{3,2,1,0:T(8,128)(2,1)}, u32[]{:S(2)}) copy-start(bf16[1,2,16,512]{3,2,1,0:T(8,128)(2,1)} %param.15) | copy-start | bytes 98308
  12.0 15.4 %copy-start.2 = (bf16[2,16,32,384]{3,2,1,0:T(8,128)(2,1)}, bf16[2,16,32,384]{3,2,1,0:T(8,128)(2,1)S(1)}, u32[]{:S(2)}) copy-start(bf16[2,16,32,384]{3,2,1,0:T(8,128)(2,1)S(1)} %bitcast_multiply_fusion) | copy-start | bytes 2359300
  13.0 5.8 %collective-permute-start.1 = (bf16[1,24832]{1,0:T(2,128)(2,1)S(1)}, bf16[1,24832]{1,0:T(2,128)(2,1)S(1)}, u32[]{:S(2)}, u32[]{:S(2)}) collective-permute-start(bf16[1,24832]{1,0:T(2,128)(2,1)S(1)} %pad_maximum_fusion.18), channel_id=1, source_target_pairs={{0,6},{1,7},{2,0},{3,1},{4,2},{5,3},{6,4},{7,5},{8,14},{9,15},{10,... | collective-permute-start | bytes 149000 | tf_op jit(solution)/shard_map/ppermute | solution.py:106
  19.0 4.6 %collective-permute-start.2 = (bf16[1,49664]{1,0:T(2,128)(2,1)S(1)}, bf16[1,49664]{1,0:T(2,128)(2,1)S(1)}, u32[]{:S(2)}, u32[]{:S(2)}) collective-permute-start(bf16[1,49664]{1,0:T(2,128)(2,1)S(1)} %pad_maximum_fusion.11), channel_id=1, source_target_pairs={{0,4},{1,5},{2,6},{3,7},{4,0},{5,1},{6,2},{7,3},{8,12},{9,13},{10,... | collective-permute-start | bytes 297992 | tf_op jit(solution)/shard_map/ppermute | solution.py:106
  29.6 29.2 %slice-start = ((bf16[2,16,32,384]{3,2,1,0:T(8,128)(2,1)}), bf16[1,16,32,384]{3,2,1,0:T(8,128)(2,1)S(1)}, s32[]{:S(2)}) async-start(bf16[2,16,32,384]{3,2,1,0:T(8,128)(2,1)} %copy-done.2), calls=%async_computation | async-start | bytes 786432 | tf_op jit(solution)/shard_map/slice | solution.py:29
  55.2 5.1 %collective-permute-start.3 = (bf16[3,1,32,16]{3,2,1,0:T(8,128)(2,1)S(1)}, bf16[3,1,32,16]{3,2,1,0:T(8,128)(2,1)S(1)}, u32[]{:S(2)}, u32[]{:S(2)}) collective-permute-start(bf16[3,1,32,16]{3,2,1,0:T(8,128)(2,1)S(1)} %get-tuple-element.84), channel_id=1, source_target_pairs={{0,4},{1,5},{2,6},{3,7},{8,12},{9,13},{10,14},{11,15},{16,20},{17,... | collective-permute-start | bytes 9224 | tf_op jit(solution)/shard_map/ppermute | solution.py:16
  57.5 4.6 %collective-permute-start.4 = (bf16[3,1,32,16]{3,2,1,0:T(8,128)(2,1)S(1)}, bf16[3,1,32,16]{3,2,1,0:T(8,128)(2,1)S(1)}, u32[]{:S(2)}, u32[]{:S(2)}) collective-permute-start(bf16[3,1,32,16]{3,2,1,0:T(8,128)(2,1)S(1)} %get-tuple-element.85), channel_id=1, source_target_pairs={{4,0},{5,1},{6,2},{7,3},{12,8},{13,9},{14,10},{15,11},{20,16},{21,... | collective-permute-start | bytes 9224 | tf_op jit(solution)/shard_map/ppermute | solution.py:17
  62.3 12.3 %collective-permute-start.6 = (bf16[3,18,1,16]{3,2,1,0:T(2,128)(2,1)S(1)}, bf16[3,18,1,16]{3,2,1,0:T(2,128)(2,1)S(1)}, u32[]{:S(2)}, u32[]{:S(2)}) collective-permute-start(bf16[3,18,1,16]{3,2,1,0:T(2,128)(2,1)S(1)} %get-tuple-element.68), channel_id=1, source_target_pairs={{1,0},{2,1},{3,2},{5,4},{6,5},{7,6},{9,8},{10,9},{11,10},{13,12},{... | collective-permute-start | bytes 5192 | tf_op jit(solution)/shard_map/ppermute | solution.py:17
  69.2 6.3 %collective-permute-start.5 = (bf16[3,18,1,16]{3,2,1,0:T(2,128)(2,1)S(1)}, bf16[3,18,1,16]{3,2,1,0:T(2,128)(2,1)S(1)}, u32[]{:S(2)}, u32[]{:S(2)}) collective-permute-start(bf16[3,18,1,16]{3,2,1,0:T(2,128)(2,1)S(1)} %get-tuple-element.69), channel_id=1, source_target_pairs={{0,1},{1,2},{2,3},{4,5},{5,6},{6,7},{8,9},{9,10},{10,11},{12,13},{... | collective-permute-start | bytes 5192 | tf_op jit(solution)/shard_map/ppermute | solution.py:16
  77.2 2.0 %copy-start.18 = (bf16[512,432]{0,1:T(8,128)(2,1)S(1)}, bf16[512,432]{0,1:T(8,128)(2,1)}, u32[]{:S(2)}) copy-start(bf16[512,432]{0,1:T(8,128)(2,1)} %constant_dynamic-update-slice_fusion.34) | copy-start | bytes 1327108
  80.1 18.4 %slice-start.1 = ((s8[7962624]{0:T(1024)(128)(4,1)}), s8[4194304]{0:T(1024)(128)(4,1)S(1)}, s32[]{:S(2)}) async-start(s8[7962624]{0:T(1024)(128)(4,1)} %bitcast.187), calls=%async_computation.1 | async-start | bytes 8388608
  80.6 4.2 %collective-permute-start.7 = (bf16[3,1,32,384]{3,2,1,0:T(8,128)(2,1)S(1)}, bf16[3,1,32,384]{3,2,1,0:T(8,128)(2,1)S(1)}, u32[]{:S(2)}, u32[]{:S(2)}) collective-permute-start(bf16[3,1,32,384]{3,2,1,0:T(8,128)(2,1)S(1)} %get-tuple-element.45), channel_id=1, source_target_pairs={{0,4},{1,5},{2,6},{3,7},{8,12},{9,13},{10,14},{11,15},{16,20},{17,... | collective-permute-start | bytes 221192 | tf_op jit(solution)/shard_map/ppermute | solution.py:16
  82.1 5.1 %collective-permute-start.8 = (bf16[3,1,32,384]{3,2,1,0:T(8,128)(2,1)S(1)}, bf16[3,1,32,384]{3,2,1,0:T(8,128)(2,1)S(1)}, u32[]{:S(2)}, u32[]{:S(2)}) collective-permute-start(bf16[3,1,32,384]{3,2,1,0:T(8,128)(2,1)S(1)} %get-tuple-element.46), channel_id=1, source_target_pairs={{4,0},{5,1},{6,2},{7,3},{12,8},{13,9},{14,10},{15,11},{20,16},{21,... | collective-permute-start | bytes 221192 | tf_op jit(solution)/shard_map/ppermute | solution.py:17
  84.8 13.8 %slice-start.2 = ((s8[7962624]{0:T(1024)(128)(4,1)}), s8[3768320]{0:T(1024)(128)(4,1)S(1)}, s32[]{:S(2)}) async-start(s8[7962624]{0:T(1024)(128)(4,1)} %bitcast.187), calls=%async_computation.2 | async-start | bytes 7536640
  89.1 11.0 %collective-permute-start.10 = (bf16[3,18,1,384]{3,2,1,0:T(2,128)(2,1)S(1)}, bf16[3,18,1,384]{3,2,1,0:T(2,128)(2,1)S(1)}, u32[]{:S(2)}, u32[]{:S(2)}) collective-permute-start(bf16[3,18,1,384]{3,2,1,0:T(2,128)(2,1)S(1)} %get-tuple-element.35), channel_id=1, source_target_pairs={{1,0},{2,1},{3,2},{5,4},{6,5},{7,6},{9,8},{10,9},{11,10},{13,12},{... | collective-permute-start | bytes 124424 | tf_op jit(solution)/shard_map/ppermute | solution.py:17
  91.0 9.1 %collective-permute-start.9 = (bf16[3,18,1,384]{3,2,1,0:T(2,128)(2,1)S(1)}, bf16[3,18,1,384]{3,2,1,0:T(2,128)(2,1)S(1)}, u32[]{:S(2)}, u32[]{:S(2)}) collective-permute-start(bf16[3,18,1,384]{3,2,1,0:T(2,128)(2,1)S(1)} %get-tuple-element.34), channel_id=1, source_target_pairs={{0,1},{1,2},{2,3},{4,5},{5,6},{6,7},{8,9},{9,10},{10,11},{12,13},{... | collective-permute-start | bytes 124424 | tf_op jit(solution)/shard_map/ppermute | solution.py:16
  113.9 2.7 %collective-permute-start.11 = (bf16[1,32,384]{2,1,0:T(8,128)(2,1)S(1)}, bf16[1,32,384]{2,1,0:T(8,128)(2,1)S(1)}, u32[]{:S(2)}, u32[]{:S(2)}) collective-permute-start(bf16[1,32,384]{2,1,0:T(8,128)(2,1)S(1)} %get-tuple-element.76), channel_id=1, source_target_pairs={{0,4},{1,5},{2,6},{3,7},{8,12},{9,13},{10,14},{11,15},{16,20},{17,... | collective-permute-start | bytes 73736 | tf_op jit(solution)/shard_map/ppermute | solution.py:16
  115.4 4.6 %collective-permute-start.12 = (bf16[1,32,384]{2,1,0:T(8,128)(2,1)S(1)}, bf16[1,32,384]{2,1,0:T(8,128)(2,1)S(1)}, u32[]{:S(2)}, u32[]{:S(2)}) collective-permute-start(bf16[1,32,384]{2,1,0:T(8,128)(2,1)S(1)} %get-tuple-element.77), channel_id=1, source_target_pairs={{4,0},{5,1},{6,2},{7,3},{12,8},{13,9},{14,10},{15,11},{20,16},{21,... | collective-permute-start | bytes 73736 | tf_op jit(solution)/shard_map/ppermute | solution.py:17
  120.0 6.5 %collective-permute-start.13 = (bf16[18,1,384]{2,1,0:T(2,128)(2,1)S(1)}, bf16[18,1,384]{2,1,0:T(2,128)(2,1)S(1)}, u32[]{:S(2)}, u32[]{:S(2)}) collective-permute-start(bf16[18,1,384]{2,1,0:T(2,128)(2,1)S(1)} %get-tuple-element.48), channel_id=1, source_target_pairs={{0,1},{1,2},{2,3},{4,5},{5,6},{6,7},{8,9},{9,10},{10,11},{12,13},{... | collective-permute-start | bytes 41480 | tf_op jit(solution)/shard_map/ppermute | solution.py:16
  123.8 5.2 %collective-permute-start.14 = (bf16[18,1,384]{2,1,0:T(2,128)(2,1)S(1)}, bf16[18,1,384]{2,1,0:T(2,128)(2,1)S(1)}, u32[]{:S(2)}, u32[]{:S(2)}) collective-permute-start(bf16[18,1,384]{2,1,0:T(2,128)(2,1)S(1)} %get-tuple-element.49), channel_id=1, source_target_pairs={{1,0},{2,1},{3,2},{5,4},{6,5},{7,6},{9,8},{10,9},{11,10},{13,12},{... | collective-permute-start | bytes 41480 | tf_op jit(solution)/shard_map/ppermute | solution.py:17
  136.7 3.6 %copy-start.12 = (bf16[3456,192]{0,1:T(8,128)(2,1)S(1)}, bf16[3456,192]{0,1:T(8,128)(2,1)}, u32[]{:S(2)}) copy-start(bf16[3456,192]{0,1:T(8,128)(2,1)} %param.22) | copy-start | bytes 3981316
  146.2 3.3 %copy-start.1 = (bf16[432,384]{1,0:T(8,128)(2,1)S(1)}, bf16[432,384]{1,0:T(8,128)(2,1)}, u32[]{:S(2)}) copy-start(bf16[432,384]{1,0:T(8,128)(2,1)} %param.17) | copy-start | bytes 995332
  (14 other events, 15.9 us)
